TPU v7x, 32 devices: a whole 2x2x4 slice. The times are simulated.
32 devices in a mesh: grp: 2 (over y), src: 4 (over z), rcv: 4 (over x, core).
Axes of the slice: x: 2, y: 2, z: 4, core: 2. Of those that a mesh axis runs over, the one named last changes fastest.
Arguments:
- traces: bfloat16 [8, 1024, 2048], P(None, ('grp', 'rcv', 'src')), parts along dimension 1, may hold values from -120 to 120
- alive: int32 [8, 1024], P(None, ('grp', 'rcv', 'src')), parts along dimension 1, may hold values 0 or 1
- picks: int32 [32, 32], P(('grp', 'rcv', 'src')), parts along dimension 0, may hold values from 0 to 31, each once within a row
Outputs:
- correlations: bfloat16 [65, 256, 512], P(None, ('grp', 'src'), 'rcv'), parts along dimension 1
There are 2 independent parts, one for each index of `grp`. A program takes and returns all parts, laid end to end along the dimension named above; each array names one. Nothing has to cross between parts.
Inputs may be any that keep to these rules, and one draw needn't show every extreme that they name: `picks`: row b belongs to the channel block of 32 channels numbered b along rcv+src (rcv the slower); it orders that block's channels, and its first 8 entries name the block's virtual sources.
All inputs are finite; a program needn't handle non-finite values. No bound on the sum of `alive` on one device may be relied on, other than what follows from the above.
Results may differ from a plain program's by a relative error of at most 0.0056.
Values may be sent and summed in bfloat16 or wider, within the bound.
A program may use at most 64 MiB of HBM per device.

v0:
```python
import math

import jax
import jax.numpy as jnp
from jax import lax
from jax.sharding import PartitionSpec as P

SEGS = 8
SAMPLES = 2048
BINS = 256
LOWBIN = 16
MAXLAG = 32
SRC_DEV = 32


def dft_table():
    sample_ids = jnp.arange(SAMPLES, dtype=jnp.int32)
    bin_ids = LOWBIN + jnp.arange(BINS, dtype=jnp.int32)
    angles = jnp.mod(sample_ids[:, None] * bin_ids[None, :], SAMPLES).astype(jnp.float32) * (
        2.0 * math.pi / SAMPLES
    )
    hann_taper = 0.5 - 0.5 * jnp.cos(sample_ids.astype(jnp.float32) * (2.0 * math.pi / SAMPLES))
    joined = jnp.concatenate(
        [hann_taper[:, None] * jnp.cos(angles), -hann_taper[:, None] * jnp.sin(angles)], axis=1
    )
    return joined.astype(jnp.bfloat16)


def lag_tables():
    shifts = jnp.arange(2 * MAXLAG + 1, dtype=jnp.int32) - MAXLAG
    bin_ids = LOWBIN + jnp.arange(BINS, dtype=jnp.int32)
    angles = jnp.mod(shifts[:, None] * bin_ids[None, :], SAMPLES).astype(jnp.float32) * (
        2.0 * math.pi / SAMPLES
    )
    lag_scale = 1.0 / math.sqrt(SEGS * BINS)
    return (lag_scale * jnp.cos(angles), -lag_scale * jnp.sin(angles))


def spectra(samples, live, transform):
    seg_count, row_count = (samples.shape[0], samples.shape[1])
    raw_spec = jnp.dot(
        samples.reshape(seg_count * row_count, SAMPLES),
        transform,
        preferred_element_type=jnp.float32,
    )
    mean_square = jnp.mean(jnp.square(samples.astype(jnp.float32)), axis=-1).reshape(
        seg_count * row_count, 1
    )
    weight = live.reshape(seg_count * row_count, 1) / jnp.sqrt(SAMPLES * (mean_square + 1e-06))
    return (raw_spec * weight).reshape(seg_count, row_count, 2 * BINS).astype(jnp.bfloat16)


def correlate(sources, receivers, cosine_lag_table, sine_lag_table):
    seg_count, src_count = (sources.shape[0], sources.shape[1])
    receiver_count = receivers.shape[1]
    source_block_view = (
        sources.reshape(seg_count, src_count, 2, BINS)
        .transpose(3, 1, 0, 2)
        .reshape(BINS, src_count, 2 * seg_count)
    )
    receiver_view = receivers.reshape(seg_count, receiver_count, 2, BINS)
    real_part = receiver_view[:, :, 0, :]
    imag_part = receiver_view[:, :, 1, :]
    real_entries = (
        jnp.stack([real_part, imag_part], axis=1)
        .transpose(3, 0, 1, 2)
        .reshape(BINS, 2 * seg_count, receiver_count)
    )
    imag_entries = (
        jnp.stack([-imag_part, real_part], axis=1)
        .transpose(3, 0, 1, 2)
        .reshape(BINS, 2 * seg_count, receiver_count)
    )
    summed_result = jnp.zeros((cosine_lag_table.shape[0], src_count, receiver_count), jnp.float32)
    bin_span = BINS // 4
    for quarter in range(4):
        bin_start = quarter * bin_span
        source_slab = source_block_view[bin_start : bin_start + bin_span]
        cross_real = jnp.einsum(
            "cni,cip->cnp",
            source_slab,
            real_entries[bin_start : bin_start + bin_span],
            preferred_element_type=jnp.float32,
        )
        cross_imag = jnp.einsum(
            "cni,cip->cnp",
            source_slab,
            imag_entries[bin_start : bin_start + bin_span],
            preferred_element_type=jnp.float32,
        )
        summed_result = summed_result + jnp.einsum(
            "iy,yhp->ihp",
            cosine_lag_table[:, bin_start : bin_start + bin_span],
            cross_real,
            precision=lax.Precision.HIGHEST,
        )
        summed_result = summed_result + jnp.einsum(
            "iy,yhp->ihp",
            sine_lag_table[:, bin_start : bin_start + bin_span],
            cross_imag,
            precision=lax.Precision.HIGHEST,
        )
    return summed_result


def shards(traces, alive, picks):
    transform = dft_table()
    cosine_lag_table, sine_lag_table = lag_tables()
    pick_count = SRC_DEV // lax.axis_size("rcv")
    chosen = picks[0, :pick_count]
    masked = jnp.where(alive[:, :, None] > 0, traces, jnp.zeros_like(traces))
    source_part = jnp.take(masked, chosen, axis=1)
    source_raw = lax.all_gather(source_part, "rcv", axis=1, tiled=True)
    sources = spectra(source_raw, jnp.ones(source_raw.shape[:2], jnp.float32), transform)
    panel_piece = lax.all_gather(masked, "src", axis=1, tiled=True)
    panel_spec = spectra(panel_piece, jnp.ones(panel_piece.shape[:2], jnp.float32), transform)
    return correlate(sources, panel_spec, cosine_lag_table, sine_lag_table).astype(jnp.bfloat16)


def solution(mesh):
    return jax.shard_map(
        shards,
        mesh=mesh,
        in_specs=(
            P(None, ("grp", "rcv", "src"), None),
            P(None, ("grp", "rcv", "src")),
            P(("grp", "rcv", "src"), None),
        ),
        out_specs=P(None, ("grp", "src"), "rcv"),
        check_vma=False,
    )
```

profile of v0, /device:TPU:0, one launch (start us, length us, event | category | flops | bytes accessed | tf_op | source)
XLA Modules:
  0.0 162.0 jit_solution(4150081740275656817)
XLA Ops:
  8.6 1.8 %copy_select_fusion = bf16[8,32,2048]{2,0,1:T(8,128)(2,1)S(1)} fusion(bf16[8,32,2048]{2,1,0:T(8,128)(2,1)} %param.3, pred[8,32]{0,1:T(8,128)(4,1)S(1)} %copy.142), kind=kLoop, calls=%fused_computation.38 | loop fusion | flops 524288 | bytes 2097408 | tf_op jit(solution)/shard_map/jit(_where)/select_n | solution.py:111
  12.7 1.3 sine_multiply_fusion
  14.0 9.2 %multiply_convert_fusion.2 = (bf16[2048,256]{1,0:T(8,128)(2,1)S(1)}, bf16[2048,256]{1,0:T(8,128)(2,1)S(1)}) fusion(s32[256]{0:T(256)S(1)} %iota_add_fusion, f32[2048]{0:T(1024)S(1)} %get-tuple-element.27, f32[2048]{0:T(1024)S(1)} %get-tuple-element.28), kind=kLoop, calls=%fused_computation.12 | loop fusion | flops 9437184 | bytes 2114560 | tf_op jit(solution)/shard_map/convert
  23.2 8.3 %all-gather.3.cloned.1.call-done = bf16[8,32,2048]{2,0,1:T(8,128)(2,1)} async-done(((bf16[8,8,2048]{2,0,1:T(8,128)(2,1)}), bf16[8,32,2048]{2,0,1:T(8,128)(2,1)}) %all-gather.3.cloned.1.call-update) | async-done | bytes 1048592 | tf_op jit(solution)/shard_map/all_gather | solution.py:113
  31.5 1.5 multiply_reduce_fusion.1
  33.2 1.8 %copy.144 = bf16[8,32,2048]{2,1,0:T(8,128)(2,1)S(1)} copy(bf16[8,32,2048]{2,0,1:T(8,128)(2,1)} %all-gather.3.cloned.1.call-done) | data formatting | bytes 2097152 | tf_op jit(solution)/shard_map/all_gather | solution.py:113
  37.0 76.9 %all-gather.5.cloned.1.call-done = bf16[8,128,2048]{2,0,1:T(8,128)(2,1)} async-done(((bf16[8,32,2048]{2,0,1:T(8,128)(2,1)}), bf16[8,128,2048]{2,0,1:T(8,128)(2,1)}) %all-gather.5.cloned.1.call-update) | async-done | bytes 4194320 | tf_op jit(solution)/shard_map/all_gather | solution.py:115
  113.9 3.1 %multiply_reduce_fusion = f32[8,128]{0,1:T(8,128)S(1)} fusion(bf16[8,128,2048]{2,0,1:T(8,128)(2,1)} %all-gather.5.cloned.1.call-done), kind=kLoop, calls=%fused_computation.1 | loop fusion | flops 6290432 | bytes 4198400 | tf_op jit(solution)/shard_map/reduce_sum | solution.py:46
  117.0 4.6 %copy.147 = bf16[8,128,2048]{2,1,0:T(8,128)(2,1)S(1)} copy(bf16[8,128,2048]{2,0,1:T(8,128)(2,1)} %all-gather.5.cloned.1.call-done) | data formatting | bytes 8388608 | tf_op jit(solution)/shard_map/all_gather | solution.py:115
  121.6 2.3 %multiply_convert_fusion = bf16[1024,512]{1,0:T(8,128)(2,1)S(1)} fusion(bf16[1024,2048]{1,0:T(8,128)(2,1)S(1)} %bitcast.71, bf16[2048,256]{1,0:T(8,128)(2,1)S(1)} %copy-done.5, bf16[2048,256]{1,0:T(8,128)(2,1)S(1)} %get-tuple-element.25, f32[1024]{0:T(1024)S(1)} %rsqrt_bitcast_fusion), kind=kOutput, calls=%fused_computation.9 | convolution fusion | flops 2152726528 | bytes 7344128 | tf_op jit(solution)/shard_map/dot_general | solution.py:41
  124.3 1.7 %fusion.45 = (bf16[8,128,1,256]{3,2,1,0:T(2,128)(2,1)S(1)}, bf16[8,128,1,256]{3,2,1,0:T(2,128)(2,1)S(1)}) fusion(bf16[8,128,2,256]{3,2,1,0:T(2,128)(2,1)S(1)} %convert_element_type.66), kind=kLoop, calls=%fused_computation.94 | loop fusion | bytes 2097152 | tf_op jit(solution)/shard_map/slice | solution.py:62
  126.3 1.6 fusion.43
  129.2 1.9 %copy.171 = bf16[64,8,2,128]{3,0,2,1:T(8,128)(2,1)} copy(bf16[64,8,2,128]{0,3,1,2:T(8,128)(2,1)} %get-tuple-element.8) | data formatting | bytes 524288 | tf_op jit(solution)/shard_map/slice | solution.py:88
  132.9 1.6 fusion.44
  134.5 1.3 copy.175
  135.8 1.3 copy.167
  140.5 1.7 %fusion.17 = f32[65,32,128]{2,0,1:T(8,128)S(1)} fusion(f32[64,32,128]{2,1,0:T(8,128)S(1)} %fusion.33, f32[65,256]{0,1:T(8,128)S(1)} %copy-done.6), kind=kOutput, calls=%fused_computation.36 | convolution fusion | flops 204472320 | bytes 2146304 | tf_op jit(solution)/shard_map/iy,yhp->ihp/dot_general | solution.py:91
  142.2 1.7 %convolution_add_fusion.6 = f32[65,32,128]{2,0,1:T(8,128)S(1)} fusion(f32[65,32,128]{2,0,1:T(8,128)S(1)} %fusion.17, f32[64,32,128]{2,1,0:T(8,128)S(1)} %fusion.31, f32[65,256]{0,1:T(8,128)S(1)} %get-tuple-element.23), kind=kOutput, calls=%fused_computation.22 | convolution fusion | flops 204738560 | bytes 3325952 | tf_op jit(solution)/shard_map/iy,yhp->ihp/dot_general | solution.py:97
  143.9 1.7 %convolution_add_fusion.5 = f32[65,32,128]{2,0,1:T(8,128)S(1)} fusion(f32[65,32,128]{2,0,1:T(8,128)S(1)} %convolution_add_fusion.6, f32[64,32,128]{2,1,0:T(8,128)S(1)} %fusion.29, f32[65,256]{0,1:T(8,128)S(1)} %copy-done.6), kind=kOutput, calls=%fused_computation.21 | convolution fusion | flops 204738560 | bytes 3325952 | tf_op jit(solution)/shard_map/iy,yhp->ihp/dot_general | solution.py:91
  145.6 1.7 %convolution_add_fusion.4 = f32[65,32,128]{2,0,1:T(8,128)S(1)} fusion(f32[65,32,128]{2,0,1:T(8,128)S(1)} %convolution_add_fusion.5, f32[64,32,128]{2,1,0:T(8,128)S(1)} %fusion.27, f32[65,256]{0,1:T(8,128)S(1)} %get-tuple-element.23), kind=kOutput, calls=%fused_computation.20 | convolution fusion | flops 204738560 | bytes 3325952 | tf_op jit(solution)/shard_map/iy,yhp->ihp/dot_general | solution.py:97
  147.3 1.9 %convolution_add_fusion.3 = f32[65,32,128]{2,0,1:T(8,128)S(1)} fusion(f32[65,32,128]{2,0,1:T(8,128)S(1)} %convolution_add_fusion.4, f32[64,32,128]{2,1,0:T(8,128)S(1)} %fusion.25, f32[65,256]{0,1:T(8,128)S(1)} %copy-done.6), kind=kOutput, calls=%fused_computation.19 | convolution fusion | flops 204738560 | bytes 3325952 | tf_op jit(solution)/shard_map/iy,yhp->ihp/dot_general | solution.py:91
  149.2 1.7 %convolution_add_fusion.2 = f32[65,32,128]{2,0,1:T(8,128)S(1)} fusion(f32[65,32,128]{2,0,1:T(8,128)S(1)} %convolution_add_fusion.3, f32[64,32,128]{2,1,0:T(8,128)S(1)} %fusion.23, f32[65,256]{0,1:T(8,128)S(1)} %get-tuple-element.23), kind=kOutput, calls=%fused_computation.18 | convolution fusion | flops 204738560 | bytes 3325952 | tf_op jit(solution)/shard_map/iy,yhp->ihp/dot_general | solution.py:97
  150.9 1.7 %convolution_add_fusion.1 = f32[65,32,128]{2,0,1:T(8,128)S(1)} fusion(f32[65,32,128]{2,0,1:T(8,128)S(1)} %convolution_add_fusion.2, f32[64,32,128]{2,1,0:T(8,128)S(1)} %fusion.21, f32[65,256]{0,1:T(8,128)S(1)} %copy-done.6), kind=kOutput, calls=%fused_computation.17 | convolution fusion | flops 204738560 | bytes 3325952 | tf_op jit(solution)/shard_map/iy,yhp->ihp/dot_general | solution.py:91
  152.6 1.7 %fusion.7 = bf16[65,32,128]{2,0,1:T(8,128)(2,1)S(1)} fusion(f32[65,32,128]{2,0,1:T(8,128)S(1)} %convolution_add_fusion.1, f32[64,32,128]{2,1,0:T(8,128)S(1)} %fusion.19, f32[65,256]{0,1:T(8,128)S(1)} %get-tuple-element.23), kind=kOutput, calls=%fused_computation.24 | convolution fusion | flops 205004800 | bytes 2793472 | tf_op jit(solution)/shard_map/iy,yhp->ihp/dot_general | solution.py:97
  (59 shorter events, 14.5 us)
Async XLA Ops:
  6.5 25.0 %all-gather.3.cloned.1.call-start = ((), (), s32[]{:S(2)}) async-start(), calls=%async_computation | async-start | bytes 1310720 | tf_op jit(solution)/shard_map/all_gather | solution.py:113
  10.5 1.5 copy-start
  11.9 102.0 %all-gather.5.cloned.1.call-start = ((), (), s32[]{:S(2)}) async-start(), calls=%async_computation.1 | async-start | bytes 5242880 | tf_op jit(solution)/shard_map/all_gather | solution.py:115
  23.2 11.8 %copy-start.4 = (bf16[2048,256]{1,0:T(8,128)(2,1)}, bf16[2048,256]{1,0:T(8,128)(2,1)S(1)}, u32[]{:S(2)}) copy-start(bf16[2048,256]{1,0:T(8,128)(2,1)S(1)} %get-tuple-element.26) | copy-start | bytes 3145732
  117.0 4.6 %copy-start.5 = (bf16[2048,256]{1,0:T(8,128)(2,1)S(1)}, bf16[2048,256]{1,0:T(8,128)(2,1)}, u32[]{:S(2)}) copy-start(bf16[2048,256]{1,0:T(8,128)(2,1)} %copy-done.4) | copy-start | bytes 3145732
  134.5 3.0 %copy-start.3 = (bf16[64,8,2,128]{3,0,2,1:T(8,128)(2,1)S(1)}, bf16[64,8,2,128]{3,0,2,1:T(8,128)(2,1)}, u32[]{:S(2)}) copy-start(bf16[64,8,2,128]{3,0,2,1:T(8,128)(2,1)} %copy.155) | copy-start | bytes 786436
  137.3 1.0 copy-start.2
  137.9 1.1 copy-start.1
  139.4 1.1 copy-start.6
Sparse Core Ops, SparseCore 0:
  12.0 19.4 all-gather.2
  33.1 80.7 all-gather.4
where the time goes:
time: 163 us; the launch traced here: 162 us
  waiting for transfers between devices  85.9 us (53%)
  local copies, waits for them, and re-layouts  22.7 us (14%)
  other arithmetic  20 us (12%)
  matrix products  19.7 us (12%)
  between operations  13.8 us (8%)
    all_gather x1, waiting for transfers between devices, shards(): panel_piece = lax.all_gather(masked, 'src', axis=1, tiled=True)  76.9 us
    another operation x1, other arithmetic  9.15 us
    all_gather x1, waiting for transfers between devices, shards(): source_raw = lax.all_gather(source_part, 'rcv', axis=1, tiled=True)  8.32 us
    dot_general x4, matrix products, correlate(): jnp.einsum('iy,yhp->ihp', cosine_lag_table[:, bin_start:bin_start + bin_s...  6.93 us
    dot_general x4, matrix products, correlate(): jnp.einsum('iy,yhp->ihp', sine_lag_table[:, bin_start:bin_start + bin_spa...  6.76 us
    slice x5, local copies, waits for them, and re-layouts, correlate(): imag_entries[bin_start:bin_start + bin_span]  6.6 us
    all_gather x1, local copies, waits for them, and re-layouts, shards(): panel_piece = lax.all_gather(masked, 'src', axis=1, tiled=True)  4.6 us
    reduce_sum x2, other arithmetic, spectra(): jnp.mean(jnp.square(samples.astype(jnp.float32)), axis=-1)  4.59 us
  transfers between devices with their start and end apart: 2, of which 2 were waited for; matrix products, arithmetic and copies ran while one was open for 10% of the time, Pallas kernels for 0%

commit v1 on v0

v1 whole, which is shorter than its diff:
```python
import functools
import math

import jax
import jax.numpy as jnp
import numpy as np
from jax import lax
from jax.experimental import pallas as pl
from jax.experimental.pallas import tpu as pltpu
from jax.sharding import PartitionSpec as P

BINS = 256
LOWBIN = 16
MAXLAG = 32
LAGS = 2 * MAXLAG + 1
SRC_DEV = 32
SEGS_PER_CHUNK = 2
MESH = pl.DeviceIdType.MESH


def dft_table(samples):
    t = np.arange(samples)
    k = LOWBIN + np.arange(BINS)
    angles = ((t[:, None] * k[None, :]) % samples) * (2.0 * math.pi / samples)
    taper = (0.5 - 0.5 * np.cos(t * (2.0 * math.pi / samples)))[:, None]
    joined = np.concatenate([taper * np.cos(angles), -taper * np.sin(angles)], axis=1)
    return joined.astype(np.float32).astype(jnp.bfloat16)


def lag_tables(samples):
    tau = np.arange(MAXLAG + 1)
    k = LOWBIN + np.arange(BINS)
    angles = ((tau[:, None] * k[None, :]) % samples) * (2.0 * math.pi / samples)
    scale = 1.0 / math.sqrt(samples)
    cosine, sine = scale * np.cos(angles), -scale * np.sin(angles)
    even = np.concatenate([cosine, cosine], axis=1)
    odd = np.concatenate([sine, -sine], axis=1)
    return even.astype(np.float32), odd.astype(np.float32)


def selectors(segs, channels, picked, n_rcv):
    rows = segs * picked
    entry = np.zeros((rows, channels), np.float32)
    entry[np.arange(rows), np.arange(rows) % picked] = 1.0
    column = np.arange(segs * channels)[None, :] - (np.arange(rows) // picked)[:, None] * channels
    order = np.zeros((segs, n_rcv, picked, n_rcv, segs, picked), np.float32)
    for g in range(segs):
        for r in range(n_rcv):
            for j in range(picked):
                order[g, r, j, r, g, j] = 1.0
    total = rows * n_rcv
    return entry, column.astype(np.float32), order.reshape(total, total).astype(jnp.bfloat16)


def kernel(
    segs, n_src, n_rcv,
    traces, alive, picks, table, even, odd, entry, column, order, out,
    panel, sources, phased, total,
    right_send, right_recv, left_send, left_recv, src_send, src_recv,
):
    channels = traces.shape[0] // segs
    samples = traces.shape[1]
    width = table.shape[1]
    chunk_rows = SEGS_PER_CHUNK * channels
    chunks = segs // SEGS_PER_CHUNK
    me, ring = lax.axis_index("src"), lax.axis_index("rcv")
    lines = ((1, right_send, right_recv), (-1, left_send, left_recv))

    barrier = pltpu.get_barrier_semaphore()
    for step, _, _ in lines:
        @pl.when((me + step >= 0) & (me + step < n_src))
        def _(step=step):
            pl.semaphore_signal(barrier, inc=1, device_id={"src": me + step}, device_id_type=MESH)
    for d in range(1, n_rcv):
        pl.semaphore_signal(
            barrier, inc=1, device_id={"rcv": lax.rem(ring + d, n_rcv)}, device_id_type=MESH
        )

    def hop(step, send, recv, h, q, shard):
        rows = pl.ds(q * chunk_rows, chunk_rows)
        return pltpu.make_async_remote_copy(
            src_ref=panel.at[shard, rows], dst_ref=panel.at[shard, rows],
            send_sem=send.at[h, q], recv_sem=recv.at[h, q],
            device_id={"src": me + step}, device_id_type=MESH,
        )

    def on_sent(h, q, act):
        for step, send, recv in lines:
            shard, target = me - step * h, me + step

            @pl.when((shard >= 0) & (shard < n_src) & (target >= 0) & (target < n_src))
            def _(step=step, send=send, recv=recv, shard=shard):
                act(hop(step, send, recv, h, q, shard))

    def arrived(h, q):
        for step, send, recv in lines:
            shard = me - step * (h + 1)

            @pl.when((shard >= 0) & (shard < n_src))
            def _(step=step, send=send, recv=recv, shard=shard):
                hop(step, send, recv, h, q, shard).wait_recv()

    def swap(d, owner):
        return pltpu.make_async_remote_copy(
            src_ref=sources.at[owner], dst_ref=sources.at[owner],
            send_sem=src_send.at[d - 1], recv_sem=src_recv.at[d - 1],
            device_id={"rcv": lax.rem(ring + d, n_rcv)}, device_id_type=MESH,
        )

    diagonal = lax.broadcasted_iota(jnp.int32, (channels, channels), 0) == lax.broadcasted_iota(
        jnp.int32, (channels, channels), 1
    )
    live = jnp.concatenate(
        [
            jnp.sum(
                jnp.where(diagonal, alive[g : g + 1, :].astype(jnp.float32), 0.0),
                axis=1, keepdims=True,
            )
            for g in range(segs)
        ],
        axis=0,
    )
    for q in range(chunks):
        rows = slice(q * chunk_rows, (q + 1) * chunk_rows)
        block = traces[rows, :]
        raw = jnp.dot(block, table[...], preferred_element_type=jnp.float32)
        wide = block.astype(jnp.float32)
        mean_square = jnp.mean(wide * wide, axis=1, keepdims=True)
        weight = live[rows] / jnp.sqrt(samples * (mean_square + 1e-06))
        panel[me, rows, :] = (raw * weight).astype(jnp.bfloat16)
        if q == 0:
            neighbours = (me > 0).astype(jnp.int32) + (me < n_src - 1).astype(jnp.int32)
            pl.semaphore_wait(barrier, n_rcv - 1 + neighbours)
        on_sent(0, q, lambda copy: copy.start())

    chosen = jnp.sum(entry[...] * picks[...].astype(jnp.float32), axis=1, keepdims=True)
    one_hot = jnp.where(column[...] == chosen, 1.0, 0.0).astype(jnp.bfloat16)
    sources[ring] = jnp.dot(one_hot, panel[me], preferred_element_type=jnp.float32).astype(
        jnp.bfloat16
    )
    for d in range(1, n_rcv):
        swap(d, ring).start()
    for d in range(1, n_rcv):
        swap(d, lax.rem(ring - d + n_rcv, n_rcv)).wait_recv()
    ordered = jnp.dot(
        order[...], sources[...].reshape(order.shape[1], width), preferred_element_type=jnp.float32
    )

    base = (MAXLAG + 1) * SRC_DEV
    half = width // 2
    for q in range(chunks):
        for i in range(SEGS_PER_CHUNK):
            g = q * SEGS_PER_CHUNK + i
            block = ordered[g * SRC_DEV : (g + 1) * SRC_DEV]
            turned = jnp.concatenate([block[:, half:], block[:, :half]], axis=1)
            lanes = slice(i * width, (i + 1) * width)
            for lag in range(MAXLAG + 1):
                at = slice(lag * SRC_DEV, (lag + 1) * SRC_DEV)
                phased[q, at, lanes] = (block * even[lag : lag + 1, :]).astype(jnp.bfloat16)
            for lag in range(1, MAXLAG + 1):
                at = slice(base + (lag - 1) * SRC_DEV, base + lag * SRC_DEV)
                phased[q, at, lanes] = (turned * odd[lag : lag + 1, :]).astype(jnp.bfloat16)
        if n_src > 2:
            arrived(0, q)
            on_sent(1, q, lambda copy: copy.start())
    for h in range(1, n_src - 2):
        for q in range(chunks):
            arrived(h, q)
            on_sent(h + 1, q, lambda copy: copy.start())

    def receivers(q, i):
        if channels % 16 == 0:
            at = q * chunk_rows + i * channels
            return panel[:, at : at + channels, :].reshape(n_src * channels, width)
        block = panel[:, q * chunk_rows : (q + 1) * chunk_rows, :].astype(jnp.float32)
        block = block.reshape(n_src, SEGS_PER_CHUNK, channels, width)[:, i]
        return block.reshape(n_src * channels, width).astype(jnp.bfloat16)

    height = total.shape[0]
    part = height // 5
    for q in range(chunks):
        arrived(n_src - 2, q)
        columns = jnp.concatenate([receivers(q, i) for i in range(SEGS_PER_CHUNK)], axis=1)
        for p in range(height // part):
            at = slice(p * part, (p + 1) * part)
            product = lax.dot_general(
                phased[q, at, :], columns, (((1,), (1,)), ((), ())),
                preferred_element_type=jnp.float32,
            )
            total[at, :] = product if q == 0 else total[at, :] + product

    out[MAXLAG] = total[:SRC_DEV, :].astype(out.dtype)
    for lag in range(1, MAXLAG + 1):
        symmetric = total[lag * SRC_DEV : (lag + 1) * SRC_DEV, :]
        skew = total[base + (lag - 1) * SRC_DEV : base + lag * SRC_DEV, :]
        out[MAXLAG + lag] = (symmetric + skew).astype(out.dtype)
        out[MAXLAG - lag] = (symmetric - skew).astype(out.dtype)

    for h in range(n_src - 1):
        for q in range(chunks):
            on_sent(h, q, lambda copy: copy.wait_send())
    for d in range(1, n_rcv):
        swap(d, ring).wait_send()


def shards(traces, alive, picks):
    segs, channels, samples = traces.shape
    n_src, n_rcv = lax.axis_size("src"), lax.axis_size("rcv")
    picked = SRC_DEV // n_rcv
    chunks = segs // SEGS_PER_CHUNK
    table = dft_table(samples)
    even, odd = lag_tables(samples)
    entry, column, order = selectors(segs, channels, picked, n_rcv)
    width = 2 * BINS
    vmem = pl.BlockSpec(memory_space=pltpu.VMEM)
    dma = pltpu.SemaphoreType.DMA
    return pl.pallas_call(
        functools.partial(kernel, segs, n_src, n_rcv),
        out_shape=jax.ShapeDtypeStruct((LAGS, SRC_DEV, n_src * channels), jnp.bfloat16),
        in_specs=[vmem] * 9,
        out_specs=vmem,
        scratch_shapes=[
            pltpu.VMEM((n_src, segs * channels, width), jnp.bfloat16),
            pltpu.VMEM((n_rcv, segs * picked, width), jnp.bfloat16),
            pltpu.VMEM((chunks, LAGS * SRC_DEV, SEGS_PER_CHUNK * width), jnp.bfloat16),
            pltpu.VMEM((LAGS * SRC_DEV, n_src * channels), jnp.float32),
            dma((n_src - 1, chunks)), dma((n_src - 1, chunks)),
            dma((n_src - 1, chunks)), dma((n_src - 1, chunks)),
            dma((n_rcv - 1,)), dma((n_rcv - 1,)),
        ],
        compiler_params=pltpu.CompilerParams(
            collective_id=0, has_side_effects=True, vmem_limit_bytes=48 * 1024 * 1024
        ),
        cost_estimate=pl.CostEstimate(flops=3 * 10**9, bytes_accessed=5 * 10**6, transcendentals=0),
    )(
        traces.reshape(segs * channels, samples), alive, picks,
        jnp.asarray(table), jnp.asarray(even), jnp.asarray(odd),
        jnp.asarray(entry), jnp.asarray(column), jnp.asarray(order),
    )


def solution(mesh):
    return jax.shard_map(
        shards,
        mesh=mesh,
        in_specs=(
            P(None, ("grp", "rcv", "src"), None),
            P(None, ("grp", "rcv", "src")),
            P(("grp", "rcv", "src"), None),
        ),
        out_specs=P(None, ("grp", "src"), "rcv"),
        check_vma=False,
    )
```

time: 163 us -> 36.1 us (0.22)
  waiting for transfers between devices: 85.9 us -> 0 us
  Pallas kernels: 0 us -> 26.4 us
  other arithmetic: 20 us -> 0 us
  matrix products: 19.7 us -> 0 us
  between operations: 13.8 us -> 0.02 us
  local copies, waits for them, and re-layouts: 22.7 us -> 9.23 us
    all_gather x2 -> x0, waiting for transfers between devices: 85.2 us -> none  [the longest x1 76.9 us: shards(): panel_piece = lax.all_gather(masked, 'src', axis=1, tiled=True)]
    pallas_call x0 -> x1, Pallas kernels: none -> 26.4 us  [shards(): pl.pallas_call(functools.partial(kernel, segs, n_src, n_rcv), out_shape=j...]
    dot_general x18 -> x0, matrix products: 19.7 us -> none  [the longest x4 6.93 us: correlate(): jnp.einsum('iy,yhp->ihp', cosine_lag_table[:, bin_start:bin_start + bin_s...]
    slice x16 -> x0, local copies, waits for them, and re-layouts: 14 us -> none  [the longest x5 6.6 us: correlate(): imag_entries[bin_start:bin_start + bin_span]]
    another operation x1 -> x0, other arithmetic: 9.15 us -> none
    unnamed x15 -> x19, local copies, waits for them, and re-layouts: 0.13 us -> 9.23 us
    all_gather x2 -> x0, local copies, waits for them, and re-layouts: 6.41 us -> none  [the longest x1 4.6 us: shards(): panel_piece = lax.all_gather(masked, 'src', axis=1, tiled=True)]
    reduce_sum x2 -> x0, other arithmetic: 4.59 us -> none  [spectra(): jnp.mean(jnp.square(samples.astype(jnp.float32)), axis=-1)]
  transfers between devices with their start and end apart: 2 -> 0, of which waited for: 2 -> 0; matrix products, arithmetic and copies ran while one was open for 10% -> 0% of each run, Pallas kernels for 0% -> 0%
where the time goes in v1:
time: 36.1 us; the launch traced here: 35.6 us
  Pallas kernels  26.4 us (73%)
  local copies, waits for them, and re-layouts  9.23 us (26%)
    pallas_call x1, Pallas kernels, shards(): pl.pallas_call(functools.partial(kernel, segs, n_src, n_rcv), out_shape=j...  26.4 us
    unnamed x19, local copies, waits for them, and re-layouts  9.23 us

profile of v1, /device:TPU:0, one launch (start us, length us, event | category | flops | bytes accessed | tf_op | source)
XLA Modules:
  0.0 35.6 jit_solution(3616912069287338309)
XLA Ops:
  0.0 0.0 copy-start
  0.0 1.2 %copy-done = bf16[8,32,2048]{2,1,0:T(8,128)(2,1)S(1)} copy-done((bf16[8,32,2048]{2,1,0:T(8,128)(2,1)S(1)}, bf16[8,32,2048]{2,1,0:T(8,128)(2,1)}, u32[]{:S(2)}) %copy-start) | copy-done | bytes 1048600
  1.2 0.0 copy-start.1
  1.2 0.7 %copy-done.1 = s32[8,32]{1,0:T(8,128)S(1)} copy-done((s32[8,32]{1,0:T(8,128)S(1)}, s32[8,32]{1,0:T(8,128)}, u32[]{:S(2)}) %copy-start.1) | copy-done | bytes 1048
  1.9 0.0 copy-start.2
  1.9 0.7 %copy-done.2 = s32[1,32]{1,0:T(1,128)S(1)} copy-done((s32[1,32]{1,0:T(1,128)S(1)}, s32[1,32]{1,0:T(1,128)}, u32[]{:S(2)}) %copy-start.2) | copy-done | bytes 152
  2.6 0.0 copy-start.3
  2.6 1.6 %copy-done.3 = bf16[2048,512]{1,0:T(8,128)(2,1)S(1)} copy-done((bf16[2048,512]{1,0:T(8,128)(2,1)S(1)}, bf16[2048,512]{1,0:T(8,128)(2,1)}, u32[]{:S(2)}) %copy-start.3) | copy-done | bytes 2097176
  4.2 0.0 copy-start.4
  4.2 0.9 %copy-done.4 = bf16[256,256]{1,0:T(8,128)(2,1)S(1)} copy-done((bf16[256,256]{1,0:T(8,128)(2,1)S(1)}, bf16[256,256]{1,0:T(8,128)(2,1)}, u32[]{:S(2)}) %copy-start.4) | copy-done | bytes 131096
  5.1 0.0 copy-start.5
  5.1 0.9 %copy-done.5 = f32[33,512]{1,0:T(8,128)S(1)} copy-done((f32[33,512]{1,0:T(8,128)S(1)}, f32[33,512]{1,0:T(8,128)}, u32[]{:S(2)}) %copy-start.5) | copy-done | bytes 67608
  6.0 0.0 copy-start.6
  6.0 0.9 %copy-done.6 = f32[33,512]{1,0:T(8,128)S(1)} copy-done((f32[33,512]{1,0:T(8,128)S(1)}, f32[33,512]{1,0:T(8,128)}, u32[]{:S(2)}) %copy-start.6) | copy-done | bytes 67608
  6.8 0.0 copy-start.7
  6.8 0.8 %copy-done.7 = f32[64,256]{1,0:T(8,128)S(1)} copy-done((f32[64,256]{1,0:T(8,128)S(1)}, f32[64,256]{1,0:T(8,128)}, u32[]{:S(2)}) %copy-start.7) | copy-done | bytes 65560
  7.7 0.0 copy-start.8
  7.7 0.8 %copy-done.8 = f32[64,32]{1,0:T(8,128)S(1)} copy-done((f32[64,32]{1,0:T(8,128)S(1)}, f32[64,32]{1,0:T(8,128)}, u32[]{:S(2)}) %copy-start.8) | copy-done | bytes 8216
  8.4 26.4 %shard_map.91 = bf16[65,32,128]{2,1,0:T(8,128)(2,1)S(1)} custom-call(bf16[256,2048]{1,0:T(8,128)(2,1)S(1)} %bitcast.1, s32[8,32]{1,0:T(8,128)S(1)} %copy-done.1, s32[1,32]{1,0:T(1,128)S(1)} %copy-done.2, bf16[2048,512]{1,0:T(8,128)(2,1)S(1)} %copy-done.3, f32[33,512]{1,0:T(8,128)S(1)} %copy-done.6, f32[33,512]{1,0:T(8,128)S(1)} %copy-done.5, ...), custom_call_target="tpu_custom_call" | custom-call | flops 3000000000 | bytes 5000000 | tf_op jit(solution)/shard_map/pallas_call | solution.py:217
  34.8 0.8 %copy.11 = bf16[65,32,128]{2,1,0:T(8,128)(2,1)} copy(bf16[65,32,128]{2,1,0:T(8,128)(2,1)S(1)} %shard_map.91) | data formatting | bytes 1064960
Async XLA Ops:
  0.0 1.2 %copy-start = (bf16[8,32,2048]{2,1,0:T(8,128)(2,1)S(1)}, bf16[8,32,2048]{2,1,0:T(8,128)(2,1)}, u32[]{:S(2)}) copy-start(bf16[8,32,2048]{2,1,0:T(8,128)(2,1)} %param.9) | copy-start | bytes 3145732
  1.2 0.7 %copy-start.1 = (s32[8,32]{1,0:T(8,128)S(1)}, s32[8,32]{1,0:T(8,128)}, u32[]{:S(2)}) copy-start(s32[8,32]{1,0:T(8,128)} %alive.1) | copy-start | bytes 3076
  1.9 0.7 %copy-start.2 = (s32[1,32]{1,0:T(1,128)S(1)}, s32[1,32]{1,0:T(1,128)}, u32[]{:S(2)}) copy-start(s32[1,32]{1,0:T(1,128)} %picks.1) | copy-start | bytes 388
  2.6 1.6 %copy-start.3 = (bf16[2048,512]{1,0:T(8,128)(2,1)S(1)}, bf16[2048,512]{1,0:T(8,128)(2,1)}, u32[]{:S(2)}) copy-start(bf16[2048,512]{1,0:T(8,128)(2,1)} %constant.12.clone.table) | copy-start | bytes 6291460
  4.2 0.9 %copy-start.4 = (bf16[256,256]{1,0:T(8,128)(2,1)S(1)}, bf16[256,256]{1,0:T(8,128)(2,1)}, u32[]{:S(2)}) copy-start(bf16[256,256]{1,0:T(8,128)(2,1)} %constant.17.clone.order) | copy-start | bytes 393220
  5.1 0.9 %copy-start.5 = (f32[33,512]{1,0:T(8,128)S(1)}, f32[33,512]{1,0:T(8,128)}, u32[]{:S(2)}) copy-start(f32[33,512]{1,0:T(8,128)} %constant.14.clone.odd) | copy-start | bytes 202756
  6.0 0.9 %copy-start.6 = (f32[33,512]{1,0:T(8,128)S(1)}, f32[33,512]{1,0:T(8,128)}, u32[]{:S(2)}) copy-start(f32[33,512]{1,0:T(8,128)} %constant.13.clone.even) | copy-start | bytes 202756
  6.8 0.8 %copy-start.7 = (f32[64,256]{1,0:T(8,128)S(1)}, f32[64,256]{1,0:T(8,128)}, u32[]{:S(2)}) copy-start(f32[64,256]{1,0:T(8,128)} %constant.16.clone.column) | copy-start | bytes 196612
  7.7 0.8 %copy-start.8 = (f32[64,32]{1,0:T(8,128)S(1)}, f32[64,32]{1,0:T(8,128)}, u32[]{:S(2)}) copy-start(f32[64,32]{1,0:T(8,128)} %constant.15.clone.entry) | copy-start | bytes 24580

commit v2 on v1

--- a/solution.py
+++ b/solution.py
@@ -14,7 +14,6 @@
 MAXLAG = 32
 LAGS = 2 * MAXLAG + 1
 SRC_DEV = 32
-SEGS_PER_CHUNK = 2
 MESH = pl.DeviceIdType.MESH
 
 
@@ -53,16 +52,32 @@
 
 
 def kernel(
-    segs, n_src, n_rcv,
-    traces, alive, picks, table, even, odd, entry, column, order, out,
+    segs, n_src, n_rcv, per_chunk,
+    traces_hbm, alive_hbm, picks_hbm, table_hbm, even_hbm, odd_hbm, entry_hbm, column_hbm, order_hbm,
+    out,
+    traces, alive, picks, table, even, odd, entry, column, order,
     panel, sources, phased, total,
-    right_send, right_recv, left_send, left_recv, src_send, src_recv,
+    right_send, right_recv, left_send, left_recv, src_send, src_recv, load_sem,
 ):
     channels = traces.shape[0] // segs
     samples = traces.shape[1]
     width = table.shape[1]
-    chunk_rows = SEGS_PER_CHUNK * channels
-    chunks = segs // SEGS_PER_CHUNK
+    chunk_rows = per_chunk * channels
+    chunks = segs // per_chunk
+    first = segs * channels // 4
+    middle = samples // 2
+    pairs = (
+        (traces_hbm.at[pl.ds(0, first)], traces.at[pl.ds(0, first)]),
+        (table_hbm.at[pl.ds(0, middle)], table.at[pl.ds(0, middle)]),
+        (table_hbm.at[pl.ds(middle, middle)], table.at[pl.ds(middle, middle)]),
+        (alive_hbm, alive),
+        (traces_hbm.at[pl.ds(first, 3 * first)], traces.at[pl.ds(first, 3 * first)]),
+        (picks_hbm, picks), (entry_hbm, entry), (column_hbm, column), (order_hbm, order),
+        (even_hbm, even), (odd_hbm, odd),
+    )
+    loads = [pltpu.make_async_copy(a, b, load_sem.at[i]) for i, (a, b) in enumerate(pairs)]
+    for load in loads:
+        load.start()
     me, ring = lax.axis_index("src"), lax.axis_index("rcv")
     lines = ((1, right_send, right_recv), (-1, left_send, left_recv))
 
@@ -110,29 +125,46 @@
     diagonal = lax.broadcasted_iota(jnp.int32, (channels, channels), 0) == lax.broadcasted_iota(
         jnp.int32, (channels, channels), 1
     )
-    live = jnp.concatenate(
-        [
-            jnp.sum(
-                jnp.where(diagonal, alive[g : g + 1, :].astype(jnp.float32), 0.0),
-                axis=1, keepdims=True,
-            )
-            for g in range(segs)
-        ],
-        axis=0,
-    )
-    for q in range(chunks):
-        rows = slice(q * chunk_rows, (q + 1) * chunk_rows)
+    def spectrum(start, stop):
+        rows = slice(start, stop)
         block = traces[rows, :]
-        raw = jnp.dot(block, table[...], preferred_element_type=jnp.float32)
+        raw = jnp.dot(block[:, :middle], table[:middle, :], preferred_element_type=jnp.float32)
+        if start == 0:
+            loads[2].wait()
+        raw = raw + jnp.dot(
+            block[:, middle:], table[middle:, :], preferred_element_type=jnp.float32
+        )
         wide = block.astype(jnp.float32)
         mean_square = jnp.mean(wide * wide, axis=1, keepdims=True)
-        weight = live[rows] / jnp.sqrt(samples * (mean_square + 1e-06))
+        if start == 0:
+            loads[3].wait()
+        live = jnp.concatenate(
+            [
+                jnp.sum(
+                    jnp.where(diagonal, alive[g : g + 1, :].astype(jnp.float32), 0.0),
+                    axis=1, keepdims=True,
+                )
+                for g in range(start // channels, stop // channels)
+            ],
+            axis=0,
+        )
+        weight = live / jnp.sqrt(samples * (mean_square + 1e-06))
         panel[me, rows, :] = (raw * weight).astype(jnp.bfloat16)
-        if q == 0:
-            neighbours = (me > 0).astype(jnp.int32) + (me < n_src - 1).astype(jnp.int32)
-            pl.semaphore_wait(barrier, n_rcv - 1 + neighbours)
+
+    loads[0].wait()
+    loads[1].wait()
+    spectrum(0, first)
+    neighbours = (me > 0).astype(jnp.int32) + (me < n_src - 1).astype(jnp.int32)
+    pl.semaphore_wait(barrier, n_rcv - 1 + neighbours)
+    for q in range(chunks // 4):
         on_sent(0, q, lambda copy: copy.start())
-
+    loads[4].wait()
+    spectrum(first, 4 * first)
+    for q in range(chunks // 4, chunks):
+        on_sent(0, q, lambda copy: copy.start())
+
+    for load in loads[5:]:
+        load.wait()
     chosen = jnp.sum(entry[...] * picks[...].astype(jnp.float32), axis=1, keepdims=True)
     one_hot = jnp.where(column[...] == chosen, 1.0, 0.0).astype(jnp.bfloat16)
     sources[ring] = jnp.dot(one_hot, panel[me], preferred_element_type=jnp.float32).astype(
@@ -149,17 +181,16 @@
     base = (MAXLAG + 1) * SRC_DEV
     half = width // 2
     for q in range(chunks):
-        for i in range(SEGS_PER_CHUNK):
-            g = q * SEGS_PER_CHUNK + i
+        for g in range(q * per_chunk, (q + 1) * per_chunk):
             block = ordered[g * SRC_DEV : (g + 1) * SRC_DEV]
             turned = jnp.concatenate([block[:, half:], block[:, :half]], axis=1)
-            lanes = slice(i * width, (i + 1) * width)
+            lanes = slice(g * width, (g + 1) * width)
             for lag in range(MAXLAG + 1):
                 at = slice(lag * SRC_DEV, (lag + 1) * SRC_DEV)
-                phased[q, at, lanes] = (block * even[lag : lag + 1, :]).astype(jnp.bfloat16)
+                phased[at, lanes] = (block * even[lag : lag + 1, :]).astype(jnp.bfloat16)
             for lag in range(1, MAXLAG + 1):
                 at = slice(base + (lag - 1) * SRC_DEV, base + lag * SRC_DEV)
-                phased[q, at, lanes] = (turned * odd[lag : lag + 1, :]).astype(jnp.bfloat16)
+                phased[at, lanes] = (turned * odd[lag : lag + 1, :]).astype(jnp.bfloat16)
         if n_src > 2:
             arrived(0, q)
             on_sent(1, q, lambda copy: copy.start())
@@ -168,33 +199,52 @@
             arrived(h, q)
             on_sent(h + 1, q, lambda copy: copy.start())
 
-    def receivers(q, i):
+    def receivers(g):
         if channels % 16 == 0:
-            at = q * chunk_rows + i * channels
-            return panel[:, at : at + channels, :].reshape(n_src * channels, width)
+            return panel[:, g * channels : (g + 1) * channels, :].reshape(n_src * channels, width)
+        q, i = g // per_chunk, g % per_chunk
         block = panel[:, q * chunk_rows : (q + 1) * chunk_rows, :].astype(jnp.float32)
-        block = block.reshape(n_src, SEGS_PER_CHUNK, channels, width)[:, i]
+        block = block.reshape(n_src, per_chunk, channels, width)[:, i]
         return block.reshape(n_src * channels, width).astype(jnp.bfloat16)
 
-    height = total.shape[0]
-    part = height // 5
+    def product(rows, g0, columns):
+        return lax.dot_general(
+            phased[rows, g0 * width : g0 * width + columns.shape[1]], columns,
+            (((1,), (1,)), ((), ())), preferred_element_type=jnp.float32,
+        )
+
+    part = total.shape[0] // 5
+    g0 = 0
     for q in range(chunks):
         arrived(n_src - 2, q)
-        columns = jnp.concatenate([receivers(q, i) for i in range(SEGS_PER_CHUNK)], axis=1)
-        for p in range(height // part):
-            at = slice(p * part, (p + 1) * part)
-            product = lax.dot_general(
-                phased[q, at, :], columns, (((1,), (1,)), ((), ())),
-                preferred_element_type=jnp.float32,
-            )
-            total[at, :] = product if q == 0 else total[at, :] + product
-
-    out[MAXLAG] = total[:SRC_DEV, :].astype(out.dtype)
-    for lag in range(1, MAXLAG + 1):
-        symmetric = total[lag * SRC_DEV : (lag + 1) * SRC_DEV, :]
-        skew = total[base + (lag - 1) * SRC_DEV : base + lag * SRC_DEV, :]
-        out[MAXLAG + lag] = (symmetric + skew).astype(out.dtype)
-        out[MAXLAG - lag] = (symmetric - skew).astype(out.dtype)
+        g1 = (q + 1) * per_chunk
+        if g1 - g0 < 2 and q < chunks - 2:
+            continue
+        columns = jnp.concatenate([receivers(g) for g in range(g0, g1)], axis=1)
+        if q < chunks - 1:
+            for p in range(5):
+                at = slice(p * part, (p + 1) * part)
+                value = product(at, g0, columns)
+                total[at, :] = value if g0 == 0 else total[at, :] + value
+            g0 = g1
+
+    group = MAXLAG // 4
+    for p in range(4):
+        lag0 = 0 if p == 0 else 1 + p * group
+        even_at = slice(lag0 * SRC_DEV, (1 + (p + 1) * group) * SRC_DEV)
+        odd_at = slice(base + p * group * SRC_DEV, base + (p + 1) * group * SRC_DEV)
+        symmetric = total[even_at, :] + product(even_at, g0, columns)
+        skew = total[odd_at, :] + product(odd_at, g0, columns)
+        for lag in range(lag0, 1 + (p + 1) * group):
+            i = lag - lag0
+            e = symmetric[i * SRC_DEV : (i + 1) * SRC_DEV]
+            if lag == 0:
+                out[MAXLAG] = e.astype(out.dtype)
+                continue
+            i = lag - 1 - p * group
+            o = skew[i * SRC_DEV : (i + 1) * SRC_DEV]
+            out[MAXLAG + lag] = (e + o).astype(out.dtype)
+            out[MAXLAG - lag] = (e - o).astype(out.dtype)
 
     for h in range(n_src - 1):
         for q in range(chunks):
@@ -207,36 +257,39 @@
     segs, channels, samples = traces.shape
     n_src, n_rcv = lax.axis_size("src"), lax.axis_size("rcv")
     picked = SRC_DEV // n_rcv
-    chunks = segs // SEGS_PER_CHUNK
+    per_chunk = max(1, 16 // channels)
+    chunks = segs // per_chunk
     table = dft_table(samples)
     even, odd = lag_tables(samples)
     entry, column, order = selectors(segs, channels, picked, n_rcv)
     width = 2 * BINS
     vmem = pl.BlockSpec(memory_space=pltpu.VMEM)
     dma = pltpu.SemaphoreType.DMA
+    operands = (
+        traces.reshape(segs * channels, samples), alive, picks,
+        jnp.asarray(table), jnp.asarray(even), jnp.asarray(odd),
+        jnp.asarray(entry), jnp.asarray(column), jnp.asarray(order),
+    )
     return pl.pallas_call(
-        functools.partial(kernel, segs, n_src, n_rcv),
+        functools.partial(kernel, segs, n_src, n_rcv, per_chunk),
         out_shape=jax.ShapeDtypeStruct((LAGS, SRC_DEV, n_src * channels), jnp.bfloat16),
-        in_specs=[vmem] * 9,
+        in_specs=[pl.BlockSpec(memory_space=pltpu.HBM)] * len(operands),
         out_specs=vmem,
-        scratch_shapes=[
+        scratch_shapes=[pltpu.VMEM(a.shape, a.dtype) for a in operands]
+        + [
             pltpu.VMEM((n_src, segs * channels, width), jnp.bfloat16),
             pltpu.VMEM((n_rcv, segs * picked, width), jnp.bfloat16),
-            pltpu.VMEM((chunks, LAGS * SRC_DEV, SEGS_PER_CHUNK * width), jnp.bfloat16),
+            pltpu.VMEM((LAGS * SRC_DEV, segs * width), jnp.bfloat16),
             pltpu.VMEM((LAGS * SRC_DEV, n_src * channels), jnp.float32),
             dma((n_src - 1, chunks)), dma((n_src - 1, chunks)),
             dma((n_src - 1, chunks)), dma((n_src - 1, chunks)),
-            dma((n_rcv - 1,)), dma((n_rcv - 1,)),
+            dma((n_rcv - 1,)), dma((n_rcv - 1,)), dma((len(operands) + 2,)),
         ],
         compiler_params=pltpu.CompilerParams(
-            collective_id=0, has_side_effects=True, vmem_limit_bytes=48 * 1024 * 1024
+            collective_id=0, has_side_effects=True, vmem_limit_bytes=60 * 1024 * 1024
         ),
         cost_estimate=pl.CostEstimate(flops=3 * 10**9, bytes_accessed=5 * 10**6, transcendentals=0),
-    )(
-        traces.reshape(segs * channels, samples), alive, picks,
-        jnp.asarray(table), jnp.asarray(even), jnp.asarray(odd),
-        jnp.asarray(entry), jnp.asarray(column), jnp.asarray(order),
-    )
+    )(*operands)
 
 
 def solution(mesh):

time: 36.1 us -> 29.4 us (0.81)
  local copies, waits for them, and re-layouts: 9.23 us -> 1.87 us
  Pallas kernels: 26.4 us -> 27.4 us
    unnamed x19 -> x1, local copies, waits for them, and re-layouts: 9.23 us -> 1.87 us
    pallas_call x1, Pallas kernels: 26.4 us -> 27.4 us  [shards(): pl.pallas_call(functools.partial(kernel, segs, n_src, n_rcv, per_chunk),...]
where the time goes in v2:
time: 29.4 us; the launch traced here: 29.2 us
  Pallas kernels  27.4 us (93%)
  local copies, waits for them, and re-layouts  1.87 us (6%)
    pallas_call x1, Pallas kernels, shards(): pl.pallas_call(functools.partial(kernel, segs, n_src, n_rcv, per_chunk),...  27.4 us
    unnamed x1, local copies, waits for them, and re-layouts  1.87 us

profile of v2, /device:TPU:0, one launch (start us, length us, event | category | flops | bytes accessed | tf_op | source)
XLA Modules:
  0.0 29.2 jit_solution(13852378475781543313)
XLA Ops:
  0.0 27.4 %shard_map.91 = bf16[65,32,128]{2,1,0:T(8,128)(2,1)} custom-call(bf16[256,2048]{1,0:T(8,128)(2,1)} %bitcast.1, s32[8,32]{1,0:T(8,128)} %alive_hbm.1, s32[1,32]{1,0:T(1,128)} %picks_hbm.1, bf16[2048,512]{1,0:T(8,128)(2,1)} %constant.12.clone.table_hbm, f32[33,512]{1,0:T(8,128)} %constant.13.clone.even_hbm, f32[33,512]{1,0:T(8,128)} %constant.14.clone.odd_hbm, ...), custom_call_target="tpu_custom_call" | custom-call | flops 3000000000 | bytes 5000000 | tf_op jit(solution)/shard_map/pallas_call | solution.py:273
  27.4 1.9 %copy.11 = bf16[65,32,128]{2,1,0:T(8,128)(2,1)} copy(bf16[65,32,128]{2,1,0:T(8,128)(2,1)} %shard_map.91) | data formatting | bytes 1064960
